TPU v7x, 256 devices: a whole 4x4x8 slice. The times are simulated.
256 devices in a mesh: sec: 4 (over y), tok: 16 (over x, z_hi, core), tp: 4 (over z_lo).
Axes of the slice: x: 4, y: 4, z: 8 (z_hi: 2, z_lo: 4; z = z_hi * 4 + z_lo), core: 2. Of those that a mesh axis runs over, the one named last changes fastest.
Arguments:
- roll_hidden: bfloat16 [32, 384, 8192], P('tok', None, 'tp')
- lengths: int32 [32], replicated, may hold values from 1 to 384, as said below
- norm_gain: float32 [4, 8192], P('sec'), may hold values from 0.1 to 1.9
- w_query: bfloat16 [4, 8192, 4096], P('sec', 'tok', 'tp')
- key_value_weight: bfloat16 [4, 8192, 2, 512], P('sec', 'tok', None, 'tp')
- score_head: float32 [4, 4096], P('sec', 'tp'), may hold values from -1.2 to 1.2
Outputs:
- joined: float32 [4, 6144], P(None, 'tok')
- advantage: float32 [6144], P('tok')
Inputs may be any that keep to these rules, and one draw needn't show every extreme that they name: Rollouts 2 * j and 2 * j + 1 are the ones held by index j of tok. The lengths sum to 6144, and one rollout is exactly 384 long. The sum of the lengths of the rollouts held by indices below j differs from j * 384 by less than 192 for every j, and equals 575 for j = 1.
All inputs are finite; a program needn't handle non-finite values.
Results may differ from a plain program's by a relative error of at most 0.0035.
The roundings to bfloat16 on the way count: a program that leaves them out, or rounds other values in their place, can miss the bound.
Values may be sent and summed in bfloat16 or wider, within the bound.
A program may use at most 128 MiB of HBM per device.

v0:
```python
import math

import jax
import jax.numpy as jnp
from jax import lax
from jax.sharding import PartitionSpec as P

HEAD_SIZE = 128
LOCAL_TOKENS = 384


EPSILON = 1e-05
KL_WEIGHT = 0.5


def with_halo(cells, sides, width):
    for axis, dim in sides:
        count = lax.axis_size(axis)
        ends = count - 1
        head = lax.slice_in_dim(cells, 0, width, axis=dim)
        tail = lax.slice_in_dim(cells, cells.shape[dim] - width, cells.shape[dim], axis=dim)
        cells = jnp.concatenate(
            [
                lax.ppermute(tail, axis, [(i, (i + 1) % count) for i in range(ends)]),
                cells,
                lax.ppermute(head, axis, [((i + 1) % count, i) for i in range(ends)]),
            ],
            axis=dim,
        )
    return cells


def shifted(shard, axis, by):
    devices = lax.axis_size(axis)
    pairs = [(i, i + by) for i in range(devices) if 0 <= i + by < devices]
    return lax.ppermute(shard, axis, pairs)


def owner_place(packed_pos, begins, ends):
    owner = jnp.sum((packed_pos[:, None] >= ends[None, :]).astype(jnp.int32), axis=1)
    onehot = owner[:, None] == jnp.arange(ends.shape[0], dtype=jnp.int32)[None, :]
    place = packed_pos - jnp.sum(jnp.where(onehot, begins[None, :], 0), axis=1)
    owner = jnp.where(packed_pos >= 0, owner, -1)
    return (owner, place)


def place_rollouts(rollout_rows, offsets_rel, local_lengths, tok_rows):
    buffer = jnp.zeros((3 * tok_rows,) + rollout_rows.shape[2:], rollout_rows.dtype)
    positions = jnp.arange(rollout_rows.shape[1], dtype=jnp.int32)
    for index in range(rollout_rows.shape[0]):
        live = positions < local_lengths[index]
        live = live.reshape((rollout_rows.shape[1],) + (1,) * (rollout_rows.ndim - 2))
        masked = jnp.where(live, rollout_rows[index], jnp.zeros((), rollout_rows.dtype))
        buffer = lax.dynamic_update_slice_in_dim(buffer, masked, offsets_rel[index], 0)
    return buffer


def split_spill(buffer, tok_rows):
    half_rows = tok_rows // 2
    centre = buffer[half_rows : 3 * half_rows]
    spill = jnp.concatenate([buffer[:half_rows], buffer[3 * half_rows : 4 * half_rows]], axis=0)
    return (centre, spill)


def join_spill(centre, extended, tok_rows):
    half_rows = tok_rows // 2
    return centre + jnp.concatenate([extended[:half_rows], extended[3 * half_rows :]], axis=0)


def attend(query_rows, key_rows, value_rows, q_owner, q_place, k_owner, k_place, head):
    query_count = query_rows.shape[0]
    key_count = key_rows.shape[0]
    kv_heads = key_rows.shape[1] // HEAD_SIZE
    q_heads = query_rows.shape[1] // HEAD_SIZE
    query_group = q_heads // kv_heads
    query_four_axes = query_rows.reshape(query_count, kv_heads, query_group, HEAD_SIZE)
    key_three_axes = key_rows.reshape(key_count, kv_heads, HEAD_SIZE)
    value_three_axes = value_rows.reshape(key_count, kv_heads, HEAD_SIZE)
    logits = jnp.einsum(
        "qhgd,khd->hgqk", query_four_axes, key_three_axes, preferred_element_type=jnp.float32
    ) / math.sqrt(HEAD_SIZE)
    allowed = (
        (q_owner[:, None] == k_owner[None, :])
        & (k_place[None, :] <= q_place[:, None])
        & (k_owner[None, :] >= 0)
    )
    logits = jnp.where(allowed[None, None], logits, jnp.float32(-1e30))
    peak = jnp.max(logits, axis=-1, keepdims=True)
    expo = jnp.exp(logits - peak)
    probs = (expo / jnp.sum(expo, axis=-1, keepdims=True)).astype(jnp.bfloat16)
    mixed = jnp.einsum(
        "hgqk,khd->qhgd", probs, value_three_axes, preferred_element_type=jnp.float32
    )
    return jnp.sum(mixed.reshape(query_count, q_heads * HEAD_SIZE) * head[None, :], axis=1)


def project(normalized_rows, w_query, key_value_weight):
    kv_cols = 2 * key_value_weight.shape[-1]
    pieces = (
        lax.all_gather(w_query[0], "tok", axis=0, tiled=True),
        lax.all_gather(key_value_weight[0], "tok", axis=0, tiled=True),
    )
    count = pieces[0].shape[0]
    query_part = jnp.dot(normalized_rows, pieces[0], preferred_element_type=jnp.float32)
    kv_part = jnp.dot(
        normalized_rows, pieces[1].reshape(count, kv_cols), preferred_element_type=jnp.float32
    )
    key_value_pair = kv_part
    key_value_pair = key_value_pair.astype(jnp.bfloat16)
    half_cols = kv_cols // 2
    return (
        query_part.astype(jnp.bfloat16),
        key_value_pair[:, :half_cols],
        key_value_pair[:, half_cols:],
    )


def normalize(local_rows, gain):
    gathered = lax.all_gather(local_rows, "tp", axis=1, tiled=True)
    floats = gathered.astype(jnp.float32)
    scale = lax.rsqrt(jnp.mean(floats * floats, axis=1, keepdims=True) + EPSILON)
    return (floats * scale * gain[None, :]).astype(jnp.bfloat16)


def local(roll_hidden, lengths, norm_gain, w_query, key_value_weight, score_head):
    tok_rows = LOCAL_TOKENS
    half_rows = tok_rows // 2
    roll_local = roll_hidden.shape[0]
    tok_index = lax.axis_index("tok")
    ends = jnp.cumsum(lengths)
    begins = ends - lengths
    first_roll = tok_index * roll_local
    local_lengths = lax.dynamic_slice_in_dim(lengths, first_roll, roll_local, 0)
    local_begins = lax.dynamic_slice_in_dim(begins, first_roll, roll_local, 0)
    offsets_rel = local_begins - (tok_index * tok_rows - half_rows)
    head = score_head[0]
    gain = norm_gain[0]
    buffer = place_rollouts(roll_hidden, offsets_rel, local_lengths, tok_rows)
    centre, spill = split_spill(buffer, tok_rows)
    extended = with_halo(spill, (("tok", 0),), half_rows)
    packed_rows = join_spill(centre, extended, tok_rows)
    normalized_rows = normalize(packed_rows, gain)
    query, key_rows, value_rows = project(normalized_rows, w_query, key_value_weight)
    left_k, left_v = shifted((key_rows, value_rows), "tok", 1)
    all_keys = jnp.concatenate([left_k, key_rows], axis=0)
    all_values = jnp.concatenate([left_v, value_rows], axis=0)
    q_pos = tok_index * tok_rows + jnp.arange(tok_rows, dtype=jnp.int32)
    k_pos = (tok_index - 1) * tok_rows + jnp.arange(2 * tok_rows, dtype=jnp.int32)
    q_owner, q_place = owner_place(q_pos, begins, ends)
    k_owner, k_place = owner_place(k_pos, begins, ends)
    partial_score = attend(query, all_keys, all_values, q_owner, q_place, k_owner, k_place, head)
    score = lax.psum(partial_score, "tp")
    joined = lax.all_gather(score[None, :], "sec", axis=0, tiled=True)
    advantage = joined[1] - joined[2] - KL_WEIGHT * (joined[3] - joined[0])
    return (joined, advantage)


def solution(mesh):
    in_specs = (
        P("tok", None, "tp"),
        P(),
        P("sec", None),
        P("sec", "tok", "tp"),
        P("sec", "tok", None, "tp"),
        P("sec", "tp"),
    )
    out_specs = (P(None, "tok"), P("tok"))
    return jax.shard_map(local, mesh=mesh, in_specs=in_specs, out_specs=out_specs, check_vma=False)
```

profile of v0, /device:TPU:4, one launch (start us, length us, event | category | flops | bytes accessed | tf_op | source)
XLA Modules:
  0.0 503.8 jit_solution(2371703008080060952)
XLA Ops:
  7.2 0.7 copy.21
  8.1 0.7 sub.51
  8.8 0.7 dynamic_slice.6
  9.6 0.7 fusion.50
  13.9 1.3 iota_compare_fusion.2
  15.9 2.2 bitcast_select_fusion.1
  18.1 2.7 broadcast_in_dim.87
  20.8 8.3 %dynamic_update_slice.6 = bf16[1152,2048]{1,0:T(8,128)(2,1)} dynamic-update-slice(bf16[1152,2048]{1,0:T(8,128)(2,1)} %broadcast_in_dim.87, bf16[384,2048]{1,0:T(8,128)(2,1)S(1)} %get-tuple-element.7, s32[]{:T(128)S(6)} %select_n.50, s32[]{:T(128)} %constant.21.clone.1) | dynamic-update-slice | bytes 3145732 | tf_op jit(solution)/shard_map/dynamic_update_slice | solution.py:54
  29.1 8.3 %dynamic_update_slice.7 = bf16[1152,2048]{1,0:T(8,128)(2,1)} dynamic-update-slice(bf16[1152,2048]{1,0:T(8,128)(2,1)} %dynamic_update_slice.6, bf16[384,2048]{1,0:T(8,128)(2,1)S(1)} %get-tuple-element.6, s32[]{:T(128)S(6)} %select_n.52, s32[]{:T(128)} %constant.21.clone.1) | dynamic-update-slice | bytes 3145732 | tf_op jit(solution)/shard_map/dynamic_update_slice | solution.py:54
  37.4 1.5 fusion.48
  38.9 1.9 collective-permute-start
  40.9 8.5 %collective-permute-start.1 = (bf16[192,2048]{1,0:T(8,128)(2,1)S(1)}, bf16[192,2048]{1,0:T(8,128)(2,1)S(1)}, u32[]{:S(2)}, u32[]{:S(2)}) collective-permute-start(bf16[192,2048]{1,0:T(8,128)(2,1)S(1)} %get-tuple-element.5), channel_id=1, source_target_pairs={{4,0},{8,4},{12,8},{16,12},{20,16},{24,20},{28,24},{32,28},{36,32}... | collective-permute-start | bytes 2359304 | tf_op jit(solution)/shard_map/ppermute | solution.py:26
  49.4 10.9 %collective-permute-done = bf16[192,2048]{1,0:T(8,128)(2,1)S(1)} collective-permute-done((bf16[192,2048]{1,0:T(8,128)(2,1)S(1)}, bf16[192,2048]{1,0:T(8,128)(2,1)S(1)}, u32[]{:S(2)}, u32[]{:S(2)}) %collective-permute-start) | collective-permute-done | bytes 786464 | tf_op jit(solution)/shard_map/ppermute | solution.py:24
  60.3 22.0 %collective-permute-done.1 = bf16[192,2048]{1,0:T(8,128)(2,1)S(1)} collective-permute-done((bf16[192,2048]{1,0:T(8,128)(2,1)S(1)}, bf16[192,2048]{1,0:T(8,128)(2,1)S(1)}, u32[]{:S(2)}, u32[]{:S(2)}) %collective-permute-start.1) | collective-permute-done | bytes 786464 | tf_op jit(solution)/shard_map/ppermute | solution.py:26
  82.3 3.0 slice_add_fusion
  85.4 0.7 all-gather.9.cloned.1.call-update
  86.2 0.7 all-gather.11.cloned.1.call-update
  87.3 0.8 and_and_fusion
  88.1 117.7 %all-gather.7.cloned.1.call-done = bf16[384,8192]{1,0:T(8,128)(2,1)} async-done(((bf16[384,2048]{1,0:T(8,128)(2,1)}), bf16[384,8192]{1,0:T(8,128)(2,1)}) %all-gather.7.cloned.1.call-update) | async-done | bytes 6291472 | tf_op jit(solution)/shard_map/all_gather | solution.py:119
  205.8 4.1 fusion.2
  209.9 74.2 %all-gather.9.cloned.1.call-done = bf16[1,8192,2,128]{3,2,0,1:T(2,128)(2,1)} async-done(((bf16[1,512,2,128]{3,2,0,1:T(2,128)(2,1)}), bf16[1,8192,2,128]{3,2,0,1:T(2,128)(2,1)}) %all-gather.9.cloned.1.call-update) | async-done | bytes 4194320 | tf_op jit(solution)/shard_map/all_gather | solution.py:101
  284.1 6.0 %fusion.27 = bf16[384,256]{1,0:T(8,128)(2,1)S(1)} fusion(bf16[1024,8,2,128]{3,2,1,0:T(2,128)(2,1)} %bitcast.76, bf16[384,8192]{1,0:T(8,128)(2,1)} %all-gather.7.cloned.1.call-done, f32[8192]{0:T(1024)S(1)} %bitcast.77, f32[384]{0:T(512)S(1)} %add_rsqrt_fusion), kind=kOutput, calls=%fused_computation.25 | convolution fusion | flops 1623293952 | bytes 10716672 | tf_op jit(solution)/shard_map/dot_general | solution.py:105
  290.1 2.1 collective-permute-start.3
  292.3 2.1 collective-permute-start.2
  294.4 163.5 %all-gather.11.cloned.1.call-done = bf16[1,8192,1024]{2,1,0:T(8,128)(2,1)} async-done(((bf16[1,512,1024]{2,1,0:T(8,128)(2,1)}), bf16[1,8192,1024]{2,1,0:T(8,128)(2,1)}) %all-gather.11.cloned.1.call-update) | async-done | bytes 16777232 | tf_op jit(solution)/shard_map/all_gather | solution.py:100
  457.9 12.2 %fusion.22 = bf16[48,8,8,128]{3,2,1,0:T(8,128)(2,1)S(1)} fusion(bf16[1,8192,1024]{2,1,0:T(8,128)(2,1)} %all-gather.11.cloned.1.call-done, bf16[384,8192]{1,0:T(8,128)(2,1)} %all-gather.7.cloned.1.call-done, f32[8192]{0:T(1024)S(1)} %bitcast.78, f32[384]{0:T(512)S(1)} %add_rsqrt_fusion), kind=kOutput, calls=%fused_computation.23 | convolution fusion | flops 6455427072 | bytes 23889408 | tf_op jit(solution)/shard_map/dot_general | solution.py:104
  470.1 1.7 fusion.6
  471.8 1.9 fusion.5
  473.8 2.9 fusion.14
  476.7 8.4 %psum.7 = f32[1,384]{1,0:T(1,128)S(1)} all-reduce(f32[1,384]{1,0:T(1,128)S(1)} %broadcast_in_dim.99), channel_id=1, replica_groups=mesh['sec'=4,'tok'=16,'tp'=4] {'tp'}, use_global_device_ids=true, to_apply=%region_9.10 | all-reduce | flops 384 | bytes 3072 | tf_op jit(solution)/shard_map/psum | solution.py:152
  485.1 11.0 %all-gather.2 = f32[4,1,384]{2,1,0:T(1,128)S(1)} all-gather(f32[1,1,384]{2,1,0:T(1,128)S(1)} %bitcast.74), channel_id=1, replica_groups=mesh['sec'=4,'tok'=16,'tp'=4] {'sec'}, dimensions={0}, use_global_device_ids=true | all-gather | bytes 7680 | tf_op jit(solution)/shard_map/all_gather | solution.py:153
  496.6 0.6 fusion.43
  (27 shorter events, 2.0 us)
Async XLA Ops:
  7.2 198.6 %all-gather.7.cloned.1.call-start = ((), (), s32[]{:S(2)}) async-start(), calls=%async_computation | async-start | bytes 7864320 | tf_op jit(solution)/shard_map/all_gather | solution.py:119
  38.9 21.3 %collective-permute-start = (bf16[192,2048]{1,0:T(8,128)(2,1)S(1)}, bf16[192,2048]{1,0:T(8,128)(2,1)S(1)}, u32[]{:S(2)}, u32[]{:S(2)}) collective-permute-start(bf16[192,2048]{1,0:T(8,128)(2,1)S(1)} %get-tuple-element.4), channel_id=1, source_target_pairs={{0,4},{4,8},{8,12},{12,16},{16,20},{20,24},{24,28},{28,32},{32,36}... | collective-permute-start | bytes 2359304 | tf_op jit(solution)/shard_map/ppermute | solution.py:24
  40.9 243.2 %copy-start = (f32[1,8192]{1,0:T(1,128)S(1)}, f32[1,8192]{1,0:T(1,128)}, u32[]{:S(2)}) copy-start(f32[1,8192]{1,0:T(1,128)} %param.8) | copy-start | bytes 98308
  40.9 41.4 %collective-permute-start.1 = (bf16[192,2048]{1,0:T(8,128)(2,1)S(1)}, bf16[192,2048]{1,0:T(8,128)(2,1)S(1)}, u32[]{:S(2)}, u32[]{:S(2)}) collective-permute-start(bf16[192,2048]{1,0:T(8,128)(2,1)S(1)} %get-tuple-element.5), channel_id=1, source_target_pairs={{4,0},{8,4},{12,8},{16,12},{20,16},{24,20},{28,24},{32,28},{36,32}... | collective-permute-start | bytes 2359304 | tf_op jit(solution)/shard_map/ppermute | solution.py:26
  85.4 198.7 %all-gather.9.cloned.1.call-start = ((), (), s32[]{:S(2)}) async-start(), calls=%async_computation.1 | async-start | bytes 4456448 | tf_op jit(solution)/shard_map/all_gather | solution.py:101
  86.1 371.8 %all-gather.11.cloned.1.call-start = ((), (), s32[]{:S(2)}) async-start(), calls=%async_computation.2 | async-start | bytes 17825792 | tf_op jit(solution)/shard_map/all_gather | solution.py:100
  290.1 180.0 %collective-permute-start.3 = (bf16[384,128]{1,0:T(8,128)(2,1)S(1)}, bf16[384,128]{1,0:T(8,128)(2,1)S(1)}, u32[]{:S(2)}, u32[]{:S(2)}) collective-permute-start(bf16[384,128]{1,0:T(8,128)(2,1)S(1)} %get-tuple-element.9), channel_id=1, source_target_pairs={{0,4},{4,8},{8,12},{12,16},{16,20},{20,24},{24,28},{28,32},{32,36}... | collective-permute-start | bytes 294920 | tf_op jit(solution)/shard_map/ppermute | solution.py:36
  292.3 181.5 %collective-permute-start.2 = (bf16[384,128]{1,0:T(8,128)(2,1)S(1)}, bf16[384,128]{1,0:T(8,128)(2,1)S(1)}, u32[]{:S(2)}, u32[]{:S(2)}) collective-permute-start(bf16[384,128]{1,0:T(8,128)(2,1)S(1)} %get-tuple-element.8), channel_id=1, source_target_pairs={{0,4},{4,8},{8,12},{12,16},{16,20},{20,24},{24,28},{28,32},{32,36}... | collective-permute-start | bytes 294920 | tf_op jit(solution)/shard_map/ppermute | solution.py:36
  471.8 2.0 copy-start.1
Sparse Core Ops, SparseCore 0:
  85.5 120.2 all-gather.6
  208.5 75.5 all-gather.8
  286.8 171.0 all-gather.10
where the time goes:
time: 506 us; the launch traced here: 504 us
  waiting for transfers between devices  390 us (77%)
  local copies, waits for them, and re-layouts  24.2 us (5%)
  matrix products  22.8 us (5%)
  blocking collectives  19.3 us (4%)
  between operations  17.7 us (3%)
  other arithmetic  15.2 us (3%)
  starting transfers between devices  14.8 us (3%)
    all_gather x1, waiting for transfers between devices, project(): lax.all_gather(w_query[0], 'tok', axis=0, tiled=True)  164 us
    all_gather x1, waiting for transfers between devices, normalize(): gathered = lax.all_gather(local_rows, 'tp', axis=1, tiled=True)  118 us
    all_gather x1, waiting for transfers between devices, project(): lax.all_gather(key_value_weight[0], 'tok', axis=0, tiled=True)  74.2 us
    ppermute x1, waiting for transfers between devices, with_halo(): lax.ppermute(head, axis, [((i + 1) % count, i) for i in range(ends)])  22 us
    dynamic_update_slice x2, local copies, waits for them, and re-layouts, place_rollouts(): lax.dynamic_update_slice_in_dim(buffer, masked, offsets_rel[index], 0)  16.6 us
    dot_general x1, matrix products, project(): jnp.dot(normalized_rows, pieces[0], preferred_element_type=jnp.float32)  12.2 us
    all_gather x1, blocking collectives, local(): joined = lax.all_gather(score[None, :], 'sec', axis=0, tiled=True)  11 us
    ppermute x1, waiting for transfers between devices, with_halo(): lax.ppermute(tail, axis, [(i, (i + 1) % count) for i in range(ends)])  10.9 us
  transfers between devices with their start and end apart: 7, of which 5 were waited for; matrix products, arithmetic and copies ran while one was open for 5% of the time, Pallas kernels for 0%

commit v1 on v0

v1 whole, which is shorter than its diff:
```python
import math

import jax
import jax.numpy as jnp
from jax import lax
from jax.experimental import pallas as pl
from jax.experimental.pallas import tpu as pltpu
from jax.sharding import PartitionSpec as P

HEAD_SIZE = 128
LOCAL_TOKENS = 384
HALF = LOCAL_TOKENS // 2
EPSILON = 1e-05
KL_WEIGHT = 0.5
MESH = pl.DeviceIdType.MESH

SEC = 4
TOK = 16
TP = 4
WIDTH = 8192
PIECE = 512
COLS = 256
CHUNKS = 5
BLOCK = 128
NEG = -1e30
SENDS = 15


def kernel(
    len_ref, x_ref, gain_ref, wq_ref, wkv_ref, head_ref,
    joined_ref, adv_ref,
    w, xs, ext, halo, a, an, ss, scale, bias, acc, qb, kv, oacc, parts,
    x_sem, w_sem, ws, wr, a_s, a_r, h_s, h_r, kv_s, kv_r, p_s, p_r,
):
    y = lax.axis_index("sec")
    tok = lax.axis_index("tok")
    k = lax.axis_index("tp")
    xx = tok // 4
    h = (tok // 2) % 2
    c = tok % 2
    d = 2 * c - 1
    group = y * 4 + k

    def tok_at(x_, h_, c_):
        return x_ * 4 + h_ * 2 + c_

    xd = (xx + d + 4) % 4
    xo = (xx - d + 4) % 4
    x2 = (xx + 2) % 4
    to_xd = (y, tok_at(xd, h, c), k)
    to_xo = (y, tok_at(xo, h, c), k)
    to_z = (y, tok_at(xx, 1 - h, c), k)
    to_sib = (y, tok_at(xx, h, 1 - c), k)
    to_next = (y, (tok + 1) % TOK, k)
    to_prev = (y, (tok + TOK - 1) % TOK, k)
    k1 = k + 1 - 2 * (k % 2)
    k2 = (k + 2) % 4
    k3 = 3 - k
    yd = (y + d + 4) % 4
    yo = (y - d + 4) % 4
    y2 = (y + 2) % 4
    to_yd = (yd, tok, k)
    to_yo = (yo, tok, k)

    xcopies = [
        pltpu.make_async_copy(
            x_ref.at[i, :, pl.ds(pl.multiple_of(y * PIECE, PIECE), PIECE)], xs.at[i], x_sem.at[i]
        )
        for i in range(2)
    ]
    wcopies = [pltpu.make_async_copy(wkv_ref, w.at[0, tok], w_sem.at[0])]
    for n in range(1, CHUNKS):
        wcopies.append(
            pltpu.make_async_copy(
                wq_ref.at[0, :, pl.ds((n - 1) * COLS, COLS)], w.at[n, tok], w_sem.at[n]
            )
        )
    for cp in wcopies[:1] + xcopies + wcopies[1:]:
        cp.start()

    barrier = pltpu.get_barrier_semaphore()
    for dev in (to_xd, to_xo, to_z, to_sib, to_next, to_prev):
        pl.semaphore_signal(barrier, inc=1, device_id=dev, device_id_type=MESH)

    def greet(i, carry):
        g = (group + i) % 16
        pl.semaphore_signal(barrier, inc=1, device_id=(g // 4, tok, g % 4), device_id_type=MESH)
        return carry

    lax.fori_loop(1, 16, greet, 0)
    pl.semaphore_wait(barrier, 21)

    def wcopy(n, s, slot, dev):
        return pltpu.make_async_remote_copy(
            src_ref=w.at[n, s], dst_ref=w.at[n, s], send_sem=ws.at[n, slot], recv_sem=wr.at[n, s],
            device_id=dev, device_id_type=MESH,
        )

    def wsend(n, s, slot, dev):
        wcopy(n, s, slot, dev).start()

    def wwait(n, s):
        wcopy(n, s, 0, to_sib).wait_recv()

    def own_x(n):
        wcopies[n].wait()
        wsend(n, tok, 0, to_xd)
        wsend(n, tok, 1, to_xo)

    def own_sib(n):
        wsend(n, tok, 2, to_sib)

    def own_z(n):
        wsend(n, tok, 3, to_z)

    def ring1(n, h_, base):
        s = tok_at(xd, h_, c)
        wwait(n, s)
        wsend(n, s, base, to_xo)
        wsend(n, s, base + 1, to_sib)
        s = tok_at(xo, h_, c)
        wwait(n, s)
        wsend(n, s, base + 2, to_sib)

    def ring2(n, h_, base):
        s = tok_at(x2, h_, c)
        wwait(n, s)
        wsend(n, s, base + 3, to_sib)

    def own1(n):
        ring1(n, h, 7)

    def own2(n):
        ring2(n, h, 7)

    def part0(n):
        s = tok_at(xx, 1 - h, c)
        wwait(n, s)
        wsend(n, s, 4, to_xd)
        wsend(n, s, 5, to_xo)
        wsend(n, s, 6, to_sib)

    def part1(n):
        ring1(n, 1 - h, 11)

    def part2(n):
        ring2(n, 1 - h, 11)

    def sib_wait(n):
        def step(i, carry):
            wwait(n, i * 2 + 1 - c)
            return carry

        lax.fori_loop(0, 8, step, 0)

    def acopy(q, slot, dev):
        return pltpu.make_async_remote_copy(
            src_ref=a.at[q], dst_ref=a.at[q], send_sem=a_s.at[slot], recv_sem=a_r.at[q],
            device_id=dev, device_id_type=MESH,
        )

    def square(q):
        f = a[q].astype(jnp.float32)
        f = f * f
        ss[...] += (f[:, :128] + f[:, 128:256]) + (f[:, 256:384] + f[:, 384:])

    def a_y(q, slot):
        acopy(q, slot, to_yd).start()
        acopy(q, slot + 1, to_yo).start()

    def a_z(kk, slot):
        q = kk * 4 + y
        acopy(q, 0, to_yd).wait_recv()
        a_y(q, slot)
        square(q)

    def a_fwd(kk, slot):
        q = kk * 4 + yd
        acopy(q, 0, to_yd).wait_recv()
        acopy(q, slot, to_yo).start()
        square(q)

    def a_last(kk, yy):
        q = kk * 4 + yy
        acopy(q, 0, to_yd).wait_recv()
        square(q)

    own_x(0)
    own_z(0)
    own_sib(0)
    own_x(1)

    begin0 = jnp.int32(0)
    for r in range(2 * TOK):
        begin0 = begin0 + jnp.where(r < 2 * tok, len_ref[r], 0)
    len0 = len_ref[2 * tok]
    len1 = len_ref[2 * tok + 1]
    off0 = begin0 - (tok * LOCAL_TOKENS - HALF)
    off1 = off0 + len0
    for cp in xcopies:
        cp.wait()
    for rb in range(4):
        rows = lax.broadcasted_iota(jnp.int32, (HALF, LOCAL_TOKENS), 0) + rb * HALF
        place = lax.broadcasted_iota(jnp.int32, (HALF, LOCAL_TOKENS), 1)
        diff = rows - place
        e0 = jnp.where((diff == off0) & (place < len0), 1.0, 0.0).astype(jnp.bfloat16)
        e1 = jnp.where((diff == off1) & (place < len1), 1.0, 0.0).astype(jnp.bfloat16)
        both = jnp.dot(e0, xs[0], preferred_element_type=jnp.float32)
        both = both + jnp.dot(e1, xs[1], preferred_element_type=jnp.float32)
        ext[rb] = both.astype(jnp.bfloat16)

    def hcopy(src, dst, dev):
        return pltpu.make_async_remote_copy(
            src_ref=ext.at[src], dst_ref=halo.at[dst], send_sem=h_s.at[dst], recv_sem=h_r.at[dst],
            device_id=dev, device_id_type=MESH,
        )

    to_right = hcopy(3, 0, to_next)
    to_left = hcopy(0, 1, to_prev)
    to_right.start()
    to_left.start()
    ss[...] = jnp.zeros_like(ss)
    oacc[...] = jnp.zeros_like(oacc)

    own1(0)
    own_x(2)
    own_sib(1)

    to_right.wait_recv()
    to_left.wait_recv()
    mine = k * 4 + y
    a[mine, :HALF] = ext[1] + halo[0]
    a[mine, HALF:] = ext[2] + halo[1]
    acopy(mine, 0, (y, tok, k1)).start()
    acopy(mine, 1, (y, tok, k2)).start()
    acopy(mine, 2, (y, tok, k3)).start()
    a_y(mine, 3)
    own_z(1)
    square(mine)

    def bias_block(i, carry):
        t = tok * LOCAL_TOKENS + i * BLOCK + lax.broadcasted_iota(jnp.int32, (BLOCK, BLOCK), 0)
        start = jnp.zeros((BLOCK, BLOCK), jnp.int32)
        begin = jnp.int32(0)
        for r in range(2 * TOK):
            start = jnp.where(begin <= t, begin, start)
            begin = begin + len_ref[r]
        for j in range(4):
            u = (
                (tok - 1) * LOCAL_TOKENS + i * BLOCK + j * BLOCK
                + lax.broadcasted_iota(jnp.int32, (BLOCK, BLOCK), 1)
            )
            seen = (u <= t) & (u >= start)
            bias[i, :, j * BLOCK : (j + 1) * BLOCK] = jnp.where(seen, 0.0, NEG)
        return carry

    lax.fori_loop(0, 3, bias_block, 0)

    own2(0)
    own1(1)
    own_x(3)
    own_sib(2)
    a_z(k1, 5)
    own2(1)
    own1(2)
    own_x(4)
    part0(0)
    own_z(2)
    a_z(k2, 7)
    own_sib(3)
    own2(2)
    part1(0)
    own1(3)
    a_fwd(k, 11)
    a_z(k3, 9)
    own_z(3)
    own_sib(4)
    part2(0)
    own2(3)
    own1(4)
    part0(1)
    a_fwd(k1, 12)
    own_z(4)
    own2(4)
    part1(1)
    a_fwd(k2, 13)
    part2(1)
    a_last(k, yo)
    a_last(k, y2)
    a_fwd(k3, 14)
    part0(2)
    a_last(k1, yo)
    a_last(k1, y2)
    a_last(k2, yo)
    a_last(k2, y2)
    part1(2)
    a_last(k3, yo)
    a_last(k3, y2)

    total = jnp.sum(ss[...], axis=1, keepdims=True)
    scale[...] = jnp.broadcast_to(lax.rsqrt(total * (1.0 / WIDTH) + EPSILON), scale.shape)

    def norm(q, carry):
        g = gain_ref[:, pl.ds(pl.multiple_of(q * PIECE, PIECE), PIECE)]
        sc = scale[...]
        for j in range(4):
            cols = slice(j * 128, (j + 1) * 128)
            f = a[q, :, cols].astype(jnp.float32)
            an[q, :, cols] = (f * sc * g[:, cols]).astype(jnp.bfloat16)
        return carry

    lax.fori_loop(0, 16, norm, 0)

    def project(n):
        acc[...] = jnp.zeros_like(acc)

        def step(q, carry):
            acc[...] += jnp.dot(an[q], w[n, q], preferred_element_type=jnp.float32)
            return carry

        lax.fori_loop(0, 16, step, 0)

    def attend(n):
        qb[...] = acc[...].astype(jnp.bfloat16)
        for hh in range(2):
            weight = head_ref[:, (n - 1) * COLS + hh * HEAD_SIZE : (n - 1) * COLS + (hh + 1) * HEAD_SIZE]

            def block(i, carry):
                rows = pl.ds(pl.multiple_of(i * BLOCK, BLOCK), BLOCK)
                window = pl.ds(pl.multiple_of(i * BLOCK, BLOCK), 4 * BLOCK)
                s = lax.dot_general(
                    qb[rows, hh * HEAD_SIZE : (hh + 1) * HEAD_SIZE], kv[window, :HEAD_SIZE],
                    (((1,), (1,)), ((), ())), preferred_element_type=jnp.float32,
                )
                s = s * (1.0 / math.sqrt(HEAD_SIZE)) + bias[i]
                e = jnp.exp(s - jnp.max(s, axis=1, keepdims=True))
                p = (e * (1.0 / jnp.sum(e, axis=1, keepdims=True))).astype(jnp.bfloat16)
                o = jnp.dot(p, kv[window, HEAD_SIZE:], preferred_element_type=jnp.float32)
                oacc[rows] += o * weight
                return carry

            lax.fori_loop(0, 3, block, 0)

    sib_wait(0)
    project(0)
    kv[LOCAL_TOKENS:] = acc[...].astype(jnp.bfloat16)
    kv_copy = pltpu.make_async_remote_copy(
        src_ref=kv.at[pl.ds(LOCAL_TOKENS, LOCAL_TOKENS)], dst_ref=kv.at[pl.ds(0, LOCAL_TOKENS)],
        send_sem=kv_s.at[0], recv_sem=kv_r.at[0], device_id=to_next, device_id_type=MESH,
    )
    kv_copy.start()
    part2(2)
    part0(3)
    sib_wait(1)
    project(1)
    part1(3)
    kv_copy.wait_recv()
    attend(1)
    part2(3)
    part0(4)
    sib_wait(2)
    project(2)
    part1(4)
    attend(2)
    sib_wait(3)
    project(3)
    attend(3)
    part2(4)
    sib_wait(4)
    project(4)
    attend(4)

    parts[group] = jnp.sum(oacc[...].T, axis=0, keepdims=True)

    def pcopy(i, slot):
        g = (group + i) % 16
        return pltpu.make_async_remote_copy(
            src_ref=parts.at[group], dst_ref=parts.at[group], send_sem=p_s.at[i], recv_sem=p_r.at[slot],
            device_id=(g // 4, tok, g % 4), device_id_type=MESH,
        )

    def psend(i, carry):
        pcopy(i, group).start()
        return carry

    lax.fori_loop(1, 16, psend, 0)

    def pwait(i, carry):
        g = (group + i) % 16
        pltpu.make_async_remote_copy(
            src_ref=parts.at[g], dst_ref=parts.at[g], send_sem=p_s.at[i], recv_sem=p_r.at[g],
            device_id=(g // 4, tok, g % 4), device_id_type=MESH,
        ).wait_recv()
        return carry

    lax.fori_loop(1, 16, pwait, 0)
    score = [(parts[4 * s] + parts[4 * s + 1]) + (parts[4 * s + 2] + parts[4 * s + 3]) for s in range(SEC)]
    for s in range(SEC):
        joined_ref[s : s + 1] = score[s]
    adv_ref[...] = score[1] - score[2] - KL_WEIGHT * (score[3] - score[0])

    def drain(i, carry):
        wcopy(i // SENDS, tok, i % SENDS, to_sib).wait_send()
        return carry

    lax.fori_loop(0, CHUNKS * SENDS, drain, 0)

    def drain_a(i, carry):
        acopy(mine, i, to_yd).wait_send()
        return carry

    lax.fori_loop(0, 15, drain_a, 0)
    to_right.wait_send()
    to_left.wait_send()
    kv_copy.wait_send()

    def drain_p(i, carry):
        pcopy(i, group).wait_send()
        return carry

    lax.fori_loop(1, 16, drain_p, 0)


def local(roll_hidden, lengths, norm_gain, w_query, key_value_weight, score_head):
    vmem = pl.BlockSpec(memory_space=pltpu.VMEM)
    smem = pl.BlockSpec(memory_space=pltpu.SMEM)
    hbm = pl.BlockSpec(memory_space=pl.ANY)
    dma = pltpu.SemaphoreType.DMA
    bf16, f32 = jnp.bfloat16, jnp.float32
    joined, advantage = pl.pallas_call(
        kernel,
        out_shape=(
            jax.ShapeDtypeStruct((SEC, LOCAL_TOKENS), f32),
            jax.ShapeDtypeStruct((1, LOCAL_TOKENS), f32),
        ),
        in_specs=[smem, hbm, vmem, hbm, hbm, vmem],
        out_specs=(vmem, vmem),
        scratch_shapes=[
            pltpu.VMEM((CHUNKS, TOK, PIECE, COLS), bf16),
            pltpu.VMEM((2, LOCAL_TOKENS, PIECE), bf16),
            pltpu.VMEM((4, HALF, PIECE), bf16),
            pltpu.VMEM((2, HALF, PIECE), bf16),
            pltpu.VMEM((16, LOCAL_TOKENS, PIECE), bf16),
            pltpu.VMEM((16, LOCAL_TOKENS, PIECE), bf16),
            pltpu.VMEM((LOCAL_TOKENS, 128), f32),
            pltpu.VMEM((LOCAL_TOKENS, 128), f32),
            pltpu.VMEM((3, BLOCK, 4 * BLOCK), f32),
            pltpu.VMEM((LOCAL_TOKENS, COLS), f32),
            pltpu.VMEM((LOCAL_TOKENS, COLS), bf16),
            pltpu.VMEM((2 * LOCAL_TOKENS, COLS), bf16),
            pltpu.VMEM((LOCAL_TOKENS, HEAD_SIZE), f32),
            pltpu.VMEM((16, 1, LOCAL_TOKENS), f32),
            dma((2,)), dma((CHUNKS,)),
            dma((CHUNKS, SENDS)), dma((CHUNKS, TOK)),
            dma((15,)), dma((16,)),
            dma((2,)), dma((2,)),
            dma((1,)), dma((1,)),
            dma((16,)), dma((16,)),
        ],
        compiler_params=pltpu.CompilerParams(
            collective_id=0, has_side_effects=True, vmem_limit_bytes=56 * 1024 * 1024
        ),
        name="score_rollouts",
    )(
        lengths, roll_hidden, norm_gain, w_query,
        key_value_weight.reshape(PIECE, COLS), score_head,
    )
    return (joined, advantage.reshape(LOCAL_TOKENS))


def solution(mesh):
    in_specs = (
        P("tok", None, "tp"),
        P(),
        P("sec", None),
        P("sec", "tok", "tp"),
        P("sec", "tok", None, "tp"),
        P("sec", "tp"),
    )
    out_specs = (P(None, "tok"), P("tok"))
    return jax.shard_map(local, mesh=mesh, in_specs=in_specs, out_specs=out_specs, check_vma=False)
```

time: 506 us -> 192 us (0.38)
  waiting for transfers between devices: 390 us -> 0 us
  Pallas kernels: 0 us -> 183 us
  matrix products: 22.8 us -> 0 us
  local copies, waits for them, and re-layouts: 24.2 us -> 2.96 us
  blocking collectives: 19.3 us -> 0 us
  between operations: 17.7 us -> 0.64 us
  starting transfers between devices: 14.8 us -> 0 us
  other arithmetic: 15.2 us -> 1.27 us
    all_gather x3 -> x0, waiting for transfers between devices: 355 us -> none  [the longest x1 164 us: project(): lax.all_gather(w_query[0], 'tok', axis=0, tiled=True)]
    pallas_call x0 -> x1, Pallas kernels: none -> 183 us  [local(): pl.pallas_call(kernel, out_shape=(jax.ShapeDtypeStruct((SEC, LOCAL_TOKENS...]
    ppermute x4 -> x0, waiting for transfers between devices: 32.9 us -> none  [the longest x1 22 us: with_halo(): lax.ppermute(head, axis, [((i + 1) % count, i) for i in range(ends)])]
    dot_general x4 -> x0, matrix products: 22.8 us -> none  [the longest x1 12.2 us: project(): jnp.dot(normalized_rows, pieces[0], preferred_element_type=jnp.float32)]
    dynamic_update_slice x2 -> x0, local copies, waits for them, and re-layouts: 16.6 us -> none  [place_rollouts(): lax.dynamic_update_slice_in_dim(buffer, masked, offsets_rel[index], 0)]
    ppermute x4 -> x0, starting transfers between devices: 14.7 us -> none  [the longest x1 8.51 us: with_halo(): lax.ppermute(head, axis, [((i + 1) % count, i) for i in range(ends)])]
    all_gather x1 -> x0, blocking collectives: 11 us -> none  [local(): joined = lax.all_gather(score[None, :], 'sec', axis=0, tiled=True)]
    psum x1 -> x0, blocking collectives: 8.37 us -> none  [local(): score = lax.psum(partial_score, 'tp')]
  transfers between devices with their start and end apart: 7 -> 0, of which waited for: 5 -> 0; matrix products, arithmetic and copies ran while one was open for 5% -> 0% of each run, Pallas kernels for 0% -> 0%
where the time goes in v1:
time: 192 us; the launch traced here: 188 us
  Pallas kernels  183 us (95%)
  local copies, waits for them, and re-layouts  2.96 us (2%)
    pallas_call x1, Pallas kernels, local(): pl.pallas_call(kernel, out_shape=(jax.ShapeDtypeStruct((SEC, LOCAL_TOKENS...  183 us

profile of v1, /device:TPU:4, one launch (start us, length us, event | category | flops | bytes accessed | tf_op | source)
XLA Modules:
  0.0 188.1 jit_solution(18414253512834585136)
XLA Ops:
  0.6 1.7 copy.10
  2.3 183.3 %score_rollouts.1 = (f32[4,384]{1,0:T(4,128)}, f32[1,384]{1,0:T(1,128)}) custom-call(s32[32]{0:T(128)} %len_ref.1, bf16[2,384,2048]{2,1,0:T(8,128)(2,1)} %x_ref.1, f32[1,8192]{1,0:T(1,128)} %gain_ref.1, bf16[1,512,1024]{2,1,0:T(8,128)(2,1)} %wq_ref.1, bf16[512,256]{1,0:T(8,128)(2,1)} %bitcast.5, f32[1,1024]{1,0:T(1,128)} %head_ref.1), custom_call_target="tpu_custom_call" | custom-call | tf_op jit(solution)/shard_map/score_rollouts/pallas_call | solution.py:430
  185.6 1.3 reduce
  186.8 1.3 copy.12

commit v2 on v1

v2 whole, which is shorter than its diff:
```python
import math

import jax
import jax.numpy as jnp
from jax import lax
from jax.experimental import pallas as pl
from jax.experimental.pallas import tpu as pltpu
from jax.sharding import PartitionSpec as P

HEAD_SIZE = 128
LOCAL_TOKENS = 384
HALF = LOCAL_TOKENS // 2
EPSILON = 1e-05
KL_WEIGHT = 0.5
MESH = pl.DeviceIdType.MESH

SEC = 4
TOK = 16
TP = 4
WIDTH = 8192
PIECE = 512
COLS = (256, 256, 256, 256, 128, 128)
CHUNKS = len(COLS)
BLOCK = 128
NEG = -1e30
SENDS = 15

ORDER = (
    ("halo",), ("oz", 0), ("ox", 1), ("ox", 0), ("hw",), ("o1", 1), ("ao", 2), ("ox", 3), ("ss",), ("ox", 2),
    ("ao", 1), ("o1", 3), ("os", 4), ("ay",), ("o1", 2), ("ao", 3), ("oz", 1), ("ox", 4), ("o2", 1), ("az", 2),
    ("o1", 4), ("o1b", 0), ("os", 2), ("ox", 5), ("p0", 0), ("sc",), ("o1b", 2), ("o1", 0), ("af", 2),
    ("az", 1), ("af", 1), ("nm", 0, "0"), ("o1b", 4), ("nm", 1, "o"), ("nm", 1, "d"), ("nm", 1, "0"), ("o1", 5),
    ("p1", 0), ("o2", 0), ("oz", 2), ("p0", 1), ("az", 3), ("os", 0), ("o1b", 1), ("nm", 1, "2"), ("p1b", 0),
    ("o1b", 3), ("p2", 0), ("af", 0), ("o2", 2), ("nm", 0, "o"), ("os", 3), ("oz", 3), ("nm", 2, "d"),
    ("p1", 1), ("af", 3), ("p0", 2), ("os", 1), ("nm", 2, "2"), ("nm", 3, "2"), ("nm", 3, "d"), ("p2", 1),
    ("oz", 4), ("o2", 3), ("nm", 3, "0"), ("nm", 0, "d"), ("nm", 2, "o"), ("nm", 2, "0"), ("nm", 3, "o"),
    ("nm", 0, "2"), ("p1", 2), ("pj", 0), ("kvs",), ("o2", 5), ("p0", 3), ("o2", 4), ("p1b", 2), ("os", 5),
    ("o1b", 5), ("p1b", 1), ("p0", 4), ("pj", 1), ("oz", 5), ("p1", 3), ("p2", 2), ("bias",), ("p1b", 3),
    ("p1", 4), ("at", 1), ("p2", 3), ("pj", 2), ("p1b", 4), ("p0", 5), ("p2", 4), ("at", 2), ("pj", 3),
    ("p1", 5), ("at", 3), ("pj", 4), ("p1b", 5), ("p2", 5), ("at", 4), ("z0",), ("pj", 5, 0, 0),
    ("pj", 5, 1, 0), ("pj", 5, 0, 1), ("pj", 5, 1, 1), ("at", 5),
)


def kernel(len_ref, x_ref, gain_ref, wq_ref, wkv_ref, head_ref, out_ref, *scratch):
    w = scratch[:CHUNKS]
    (
        kvw, xs, ext, halo, a, an, sq, scale, bias, acc, kv, oacc, parts,
        x_sem, w_sem, ws, wr, a_s, a_r, h_s, h_r, kv_s, kv_r, p_s, p_r, q_s, q_r,
    ) = scratch[CHUNKS:]
    y = lax.axis_index("sec")
    tok = lax.axis_index("tok")
    k = lax.axis_index("tp")
    xx = tok // 4
    h = (tok // 2) % 2
    c = tok % 2
    d = 2 * c - 1
    group = y * 4 + k

    def tok_at(x_, h_, c_):
        return x_ * 4 + h_ * 2 + c_

    xd = (xx + d + 4) % 4
    xo = (xx - d + 4) % 4
    x2 = (xx + 2) % 4
    to_xd = (y, tok_at(xd, h, c), k)
    to_xo = (y, tok_at(xo, h, c), k)
    to_z = (y, tok_at(xx, 1 - h, c), k)
    to_sib = (y, tok_at(xx, h, 1 - c), k)
    to_next = (y, (tok + 1) % TOK, k)
    to_prev = (y, (tok + TOK - 1) % TOK, k)
    k1 = k + 1 - 2 * (k % 2)
    k2 = (k + 2) % 4
    k3 = 3 - k
    yd = (y + d + 4) % 4
    yo = (y - d + 4) % 4
    y2 = (y + 2) % 4
    to_yd = (yd, tok, k)
    to_yo = (yo, tok, k)

    xcopies = [
        pltpu.make_async_copy(
            x_ref.at[i, :, pl.ds(pl.multiple_of(y * PIECE, PIECE), PIECE)], xs.at[i], x_sem.at[i]
        )
        for i in range(2)
    ]
    wcopies = [pltpu.make_async_copy(wkv_ref.at[0], kvw, w_sem.at[0])]
    for n in range(1, CHUNKS):
        wcopies.append(
            pltpu.make_async_copy(
                wq_ref.at[0, :, pl.ds(sum(COLS[1:n]), COLS[n])], w[n].at[tok], w_sem.at[n]
            )
        )
    for cp in xcopies + wcopies:
        cp.start()

    barrier = pltpu.get_barrier_semaphore()
    for dev in (to_xd, to_xo, to_z, to_sib, to_next, to_prev):
        pl.semaphore_signal(barrier, inc=1, device_id=dev, device_id_type=MESH)

    def greet(i, carry):
        g = (group + i) % 16
        pl.semaphore_signal(barrier, inc=1, device_id=(g // 4, tok, g % 4), device_id_type=MESH)
        return carry

    lax.fori_loop(1, 16, greet, 0)

    def wcopy(n, s, slot, dev):
        return pltpu.make_async_remote_copy(
            src_ref=w[n].at[s], dst_ref=w[n].at[s], send_sem=ws.at[n, slot], recv_sem=wr.at[n, s],
            device_id=dev, device_id_type=MESH,
        )

    def wsend(n, s, slot, dev):
        wcopy(n, s, slot, dev).start()

    def wwait(n, s):
        wcopy(n, s, 0, to_sib).wait_recv()

    def forward(n, h_, base):
        s = tok_at(xd, h_, c)
        wwait(n, s)
        wsend(n, s, base, to_xo)
        wsend(n, s, base + 1, to_sib)

    def near(n, h_, base):
        s = tok_at(xo, h_, c)
        wwait(n, s)
        wsend(n, s, base + 2, to_sib)

    def far(n, h_, base):
        s = tok_at(x2, h_, c)
        wwait(n, s)
        wsend(n, s, base + 3, to_sib)

    def acopy(q, slot, dev):
        return pltpu.make_async_remote_copy(
            src_ref=a.at[q], dst_ref=a.at[q], send_sem=a_s.at[slot], recv_sem=a_r.at[q],
            device_id=dev, device_id_type=MESH,
        )

    begin0 = jnp.int32(0)
    for r in range(2 * TOK):
        begin0 = begin0 + jnp.where(r < 2 * tok, len_ref[r], 0)
    len0 = len_ref[2 * tok]
    len1 = len_ref[2 * tok + 1]
    off0 = begin0 - (tok * LOCAL_TOKENS - HALF)
    off1 = off0 + len0
    for cp in xcopies:
        cp.wait()
    for rb in range(4):
        rows = lax.broadcasted_iota(jnp.int32, (HALF, LOCAL_TOKENS), 0) + rb * HALF
        place = lax.broadcasted_iota(jnp.int32, (HALF, LOCAL_TOKENS), 1)
        diff = rows - place
        e0 = jnp.where((diff == off0) & (place < len0), 1.0, 0.0).astype(jnp.bfloat16)
        e1 = jnp.where((diff == off1) & (place < len1), 1.0, 0.0).astype(jnp.bfloat16)
        both = jnp.dot(e0, xs[0], preferred_element_type=jnp.float32)
        both = both + jnp.dot(e1, xs[1], preferred_element_type=jnp.float32)
        ext[rb] = both.astype(jnp.bfloat16)

    for cp in wcopies:
        cp.wait()
    w[0][tok, :, :HEAD_SIZE] = kvw[:, 0]
    w[0][tok, :, HEAD_SIZE:] = kvw[:, 1]
    pl.semaphore_wait(barrier, 21)

    def hcopy(src, dst, dev):
        return pltpu.make_async_remote_copy(
            src_ref=ext.at[src], dst_ref=halo.at[dst], send_sem=h_s.at[dst], recv_sem=h_r.at[dst],
            device_id=dev, device_id_type=MESH,
        )

    to_right = hcopy(3, 0, to_next)
    to_left = hcopy(0, 1, to_prev)
    oacc[...] = jnp.zeros_like(oacc)
    mine = k * 4 + y

    def exchange(buf, send, recv):
        def copy(i, g, slot):
            to = (group + i) % 16
            return pltpu.make_async_remote_copy(
                src_ref=buf.at[g], dst_ref=buf.at[g], send_sem=send.at[i], recv_sem=recv.at[slot],
                device_id=(to // 4, tok, to % 4), device_id_type=MESH,
            )

        def start(i, carry):
            copy(i, group, group).start()
            return carry

        def wait(i, carry):
            g = (group + i) % 16
            copy(i, g, g).wait_recv()
            return carry

        def drain(i, carry):
            copy(i, group, group).wait_send()
            return carry

        return [lambda f=f: lax.fori_loop(1, 16, f, 0) for f in (start, wait, drain)]

    squares_start, squares_wait, squares_drain = exchange(sq, q_s, q_r)
    parts_start, parts_wait, parts_drain = exchange(parts, p_s, p_r)

    def norm(q):
        g = gain_ref[:, pl.ds(pl.multiple_of(q * PIECE, PIECE), PIECE)]

        def rows(i, carry):
            r = pl.ds(pl.multiple_of(i * 64, 64), 64)
            sc = scale[r]
            for j in range(4):
                cols = slice(j * 128, (j + 1) * 128)
                f = a[q, r, cols].astype(jnp.float32)
                an[q, r, cols] = (f * sc * g[:, cols]).astype(jnp.bfloat16)
            return carry

        lax.fori_loop(0, 6, rows, 0)

    def sib_wait(n):
        def step(i, carry):
            wwait(n, i * 2 + 1 - c)
            return carry

        lax.fori_loop(0, 8, step, 0)

    def shards(n, h_, c_):
        total = None
        for i in range(4):
            q = tok_at(i, h_, c_)
            part = jnp.dot(an[q], w[n][q], preferred_element_type=jnp.float32)
            total = part if total is None else total + part
        acc[:, : COLS[n]] += total

    def bias_block(i, carry):
        t = tok * LOCAL_TOKENS + i * BLOCK + lax.broadcasted_iota(jnp.int32, (BLOCK, BLOCK), 0)
        start = jnp.zeros((BLOCK, BLOCK), jnp.int32)
        begin = jnp.int32(0)
        for r in range(2 * TOK):
            start = jnp.where(begin <= t, begin, start)
            begin = begin + len_ref[r]
        for j in range(4):
            u = (
                (tok - 1) * LOCAL_TOKENS + i * BLOCK + j * BLOCK
                + lax.broadcasted_iota(jnp.int32, (BLOCK, BLOCK), 1)
            )
            seen = (u <= t) & (u >= start)
            bias[i, :, j * BLOCK : (j + 1) * BLOCK] = jnp.where(seen, 0.0, NEG)
        return carry


    def attend(n):
        lanes = [slice(j, j + HEAD_SIZE) for j in range(0, COLS[n], HEAD_SIZE)]
        base = sum(COLS[1:n])
        weights = [head_ref[:, base + j.start : base + j.stop] for j in lanes]
        for i in range(3):
            rows = slice(i * BLOCK, (i + 1) * BLOCK)
            window = slice(i * BLOCK, (i + 4) * BLOCK)
            q = jnp.concatenate([acc[rows, j] for j in lanes], axis=0)
            s = lax.dot_general(
                q.astype(jnp.bfloat16), kv[window, :HEAD_SIZE],
                (((1,), (1,)), ((), ())), preferred_element_type=jnp.float32,
            )
            s = s * (math.log2(math.e) / math.sqrt(HEAD_SIZE))
            seen = bias[i]
            s = jnp.concatenate([s[m * BLOCK : (m + 1) * BLOCK] + seen for m in range(len(lanes))], axis=0)
            e = jnp.exp2(s - jnp.max(s, axis=1, keepdims=True))
            p = (e * (1.0 / jnp.sum(e, axis=1, keepdims=True))).astype(jnp.bfloat16)
            o = jnp.dot(p, kv[window, HEAD_SIZE:], preferred_element_type=jnp.float32)
            oacc[rows] += sum(o[m * BLOCK : (m + 1) * BLOCK] * weights[m] for m in range(len(lanes)))

    pieces = (k, k1, k2, k3)
    kv_copy = pltpu.make_async_remote_copy(
        src_ref=kv.at[pl.ds(LOCAL_TOKENS, LOCAL_TOKENS)], dst_ref=kv.at[pl.ds(0, LOCAL_TOKENS)],
        send_sem=kv_s.at[0], recv_sem=kv_r.at[0], device_id=to_next, device_id_type=MESH,
    )

    class Steps:
        def ox(n):
            wsend(n, tok, 0, to_xd)
            wsend(n, tok, 1, to_xo)

        def oz(n):
            wsend(n, tok, 3, to_z)

        def os(n):
            wsend(n, tok, 2, to_sib)

        def o1(n):
            forward(n, h, 7)

        def o1b(n):
            near(n, h, 7)

        def o2(n):
            far(n, h, 7)

        def p0(n):
            s = tok_at(xx, 1 - h, c)
            wwait(n, s)
            wsend(n, s, 4, to_xd)
            wsend(n, s, 5, to_xo)
            wsend(n, s, 6, to_sib)

        def p1(n):
            forward(n, 1 - h, 11)

        def p1b(n):
            near(n, 1 - h, 11)

        def p2(n):
            far(n, 1 - h, 11)

        def halo():
            to_right.start()
            to_left.start()

        def hw():
            to_right.wait_recv()
            to_left.wait_recv()
            a[mine, :HALF] = ext[1] + halo[0]
            a[mine, HALF:] = ext[2] + halo[1]

        def ay():
            acopy(mine, 3, to_yd).start()
            acopy(mine, 4, to_yo).start()

        def ao(i):
            acopy(mine, i - 1, (y, tok, pieces[i])).start()

        def az(i):
            q = pieces[i] * 4 + y
            acopy(q, 0, to_yd).wait_recv()
            acopy(q, 3 + 2 * i, to_yd).start()
            acopy(q, 4 + 2 * i, to_yo).start()

        def af(i):
            q = pieces[i] * 4 + yd
            acopy(q, 0, to_yd).wait_recv()
            acopy(q, 11 + i, to_yo).start()

        def ss():
            total = jnp.zeros((LOCAL_TOKENS, 128), jnp.float32)
            for j in range(4):
                f = a[mine, :, j * 128 : (j + 1) * 128].astype(jnp.float32)
                total = total + f * f
            sq[group] = jnp.sum(total.T, axis=0, keepdims=True)
            squares_start()

        def sc():
            squares_wait()
            total = sq[0]
            for g in range(1, 16):
                total = total + sq[g]
            row = lax.rsqrt(total * (1.0 / WIDTH) + EPSILON)
            scale[...] = jnp.broadcast_to(row, (128, LOCAL_TOKENS)).T

        def nm(i, r):
            q = pieces[i] * 4 + {"0": y, "d": yd, "o": yo, "2": y2}[r]
            if r in "o2":
                acopy(q, 0, to_yd).wait_recv()
            norm(q)

        def bias():
            lax.fori_loop(0, 3, bias_block, 0)

        def pj(n, a_=None, b_=None):
            if a_ is None:
                acc[...] = jnp.zeros_like(acc)
                sib_wait(n)

                def step(i, carry):
                    shards(n, i // 2, i % 2)
                    return carry

                lax.fori_loop(0, 4, step, 0)
                return
            h_ = h + a_ - 2 * h * a_
            c_ = c + b_ - 2 * c * b_
            if b_ == 1:
                def wait(i, carry):
                    wwait(n, tok_at(i, h_, c_))
                    return carry

                lax.fori_loop(0, 4, wait, 0)
            shards(n, h_, c_)

        def z0():
            acc[...] = jnp.zeros_like(acc)

        def kvs():
            kv[LOCAL_TOKENS:] = acc[...].astype(jnp.bfloat16)
            kv_copy.start()

        def at(n):
            if n == 1:
                kv_copy.wait_recv()
            attend(n)

    for name, *args in ORDER:
        getattr(Steps, name)(*args)

    parts[group] = jnp.sum(oacc[...].T, axis=0, keepdims=True)
    parts_start()
    parts_wait()
    score = [(parts[4 * s] + parts[4 * s + 1]) + (parts[4 * s + 2] + parts[4 * s + 3]) for s in range(SEC)]
    for s in range(SEC):
        out_ref[s : s + 1] = score[s]
    out_ref[SEC : SEC + 1] = score[1] - score[2] - KL_WEIGHT * (score[3] - score[0])

    for n in range(CHUNKS):
        def drain(i, carry):
            wcopy(n, tok, i, to_sib).wait_send()
            return carry

        lax.fori_loop(0, SENDS, drain, 0)

    def drain_a(i, carry):
        acopy(mine, i, to_yd).wait_send()
        return carry

    lax.fori_loop(0, 15, drain_a, 0)
    to_right.wait_send()
    to_left.wait_send()
    kv_copy.wait_send()

    squares_drain()
    parts_drain()


def local(roll_hidden, lengths, norm_gain, w_query, key_value_weight, score_head):
    vmem = pl.BlockSpec(memory_space=pltpu.VMEM)
    smem = pl.BlockSpec(memory_space=pltpu.SMEM)
    hbm = pl.BlockSpec(memory_space=pl.ANY)
    dma = pltpu.SemaphoreType.DMA
    bf16, f32 = jnp.bfloat16, jnp.float32
    out = pl.pallas_call(
        kernel,
        out_shape=jax.ShapeDtypeStruct((SEC + 1, LOCAL_TOKENS), f32),
        in_specs=[smem, hbm, vmem, hbm, hbm, vmem],
        out_specs=vmem,
        scratch_shapes=[
            *(pltpu.VMEM((TOK, PIECE, cols), bf16) for cols in COLS),
            pltpu.VMEM((PIECE, 2, HEAD_SIZE), bf16),
            pltpu.VMEM((2, LOCAL_TOKENS, PIECE), bf16),
            pltpu.VMEM((4, HALF, PIECE), bf16),
            pltpu.VMEM((2, HALF, PIECE), bf16),
            pltpu.VMEM((16, LOCAL_TOKENS, PIECE), bf16),
            pltpu.VMEM((16, LOCAL_TOKENS, PIECE), bf16),
            pltpu.VMEM((16, 1, LOCAL_TOKENS), f32),
            pltpu.VMEM((LOCAL_TOKENS, 128), f32),
            pltpu.VMEM((3, BLOCK, 4 * BLOCK), f32),
            pltpu.VMEM((LOCAL_TOKENS, max(COLS)), f32),
            pltpu.VMEM((2 * LOCAL_TOKENS, 2 * HEAD_SIZE), bf16),
            pltpu.VMEM((LOCAL_TOKENS, HEAD_SIZE), f32),
            pltpu.VMEM((16, 1, LOCAL_TOKENS), f32),
            dma((2,)), dma((CHUNKS,)),
            dma((CHUNKS, SENDS)), dma((CHUNKS, TOK)),
            dma((15,)), dma((16,)),
            dma((2,)), dma((2,)),
            dma((1,)), dma((1,)),
            dma((16,)), dma((16,)),
            dma((16,)), dma((16,)),
        ],
        compiler_params=pltpu.CompilerParams(
            collective_id=0, has_side_effects=True, vmem_limit_bytes=56 * 1024 * 1024
        ),
        name="score_rollouts",
    )(
        lengths, roll_hidden, norm_gain, w_query,
        key_value_weight, score_head,
    )
    return (out[:SEC], out[SEC])


def solution(mesh):
    in_specs = (
        P("tok", None, "tp"),
        P(),
        P("sec", None),
        P("sec", "tok", "tp"),
        P("sec", "tok", None, "tp"),
        P("sec", "tp"),
    )
    out_specs = (P(None, "tok"), P("tok"))
    return jax.shard_map(local, mesh=mesh, in_specs=in_specs, out_specs=out_specs, check_vma=False)
```

time: 192 us -> 158 us (0.82)
  Pallas kernels: 183 us -> 153 us
    pallas_call x1, Pallas kernels: 183 us -> 153 us  [local(): pl.pallas_call(kernel, out_shape=jax.ShapeDtypeStruct((SEC + 1, LOCAL_TOK...]
    unnamed x2 -> x0, local copies, waits for them, and re-layouts: 2.96 us -> none
    slice x0 -> x2, local copies, waits for them, and re-layouts: none -> 2.6 us  [local(): return (out[:SEC], out[SEC])]
where the time goes in v2:
time: 158 us; the launch traced here: 156 us
  Pallas kernels  153 us (97%)
  local copies, waits for them, and re-layouts  2.6 us (2%)
    pallas_call x1, Pallas kernels, local(): pl.pallas_call(kernel, out_shape=jax.ShapeDtypeStruct((SEC + 1, LOCAL_TOK...  153 us

profile of v2, /device:TPU:4, one launch (start us, length us, event | category | flops | bytes accessed | tf_op | source)
XLA Modules:
  0.0 155.9 jit_solution(5152310913905865440)
XLA Ops:
  0.6 152.7 %score_rollouts.1 = f32[5,384]{1,0:T(8,128)} custom-call(s32[32]{0:T(128)} %len_ref.1, bf16[2,384,2048]{2,1,0:T(8,128)(2,1)} %x_ref.1, f32[1,8192]{1,0:T(1,128)} %gain_ref.1, bf16[1,512,1024]{2,1,0:T(8,128)(2,1)} %wq_ref.1, bf16[1,512,2,128]{3,2,1,0:T(2,128)(2,1)} %wkv_ref.1, f32[1,1024]{1,0:T(1,128)} %head_ref.1), custom_call_target="tpu_custom_call" | custom-call | tf_op jit(solution)/shard_map/score_rollouts/pallas_call | solution.py:435
  153.3 1.3 slice_reduce_fusion
  154.6 1.3 slice.6

commit v3 on v2

--- a/solution.py
+++ b/solution.py
@@ -26,26 +26,26 @@
 SENDS = 15
 
 ORDER = (
-    ("halo",), ("oz", 0), ("ox", 1), ("ox", 0), ("hw",), ("o1", 1), ("ao", 2), ("ox", 3), ("ss",), ("ox", 2),
-    ("ao", 1), ("o1", 3), ("os", 4), ("ay",), ("o1", 2), ("ao", 3), ("oz", 1), ("ox", 4), ("o2", 1), ("az", 2),
-    ("o1", 4), ("o1b", 0), ("os", 2), ("ox", 5), ("p0", 0), ("sc",), ("o1b", 2), ("o1", 0), ("af", 2),
-    ("az", 1), ("af", 1), ("nm", 0, "0"), ("o1b", 4), ("nm", 1, "o"), ("nm", 1, "d"), ("nm", 1, "0"), ("o1", 5),
-    ("p1", 0), ("o2", 0), ("oz", 2), ("p0", 1), ("az", 3), ("os", 0), ("o1b", 1), ("nm", 1, "2"), ("p1b", 0),
-    ("o1b", 3), ("p2", 0), ("af", 0), ("o2", 2), ("nm", 0, "o"), ("os", 3), ("oz", 3), ("nm", 2, "d"),
-    ("p1", 1), ("af", 3), ("p0", 2), ("os", 1), ("nm", 2, "2"), ("nm", 3, "2"), ("nm", 3, "d"), ("p2", 1),
-    ("oz", 4), ("o2", 3), ("nm", 3, "0"), ("nm", 0, "d"), ("nm", 2, "o"), ("nm", 2, "0"), ("nm", 3, "o"),
-    ("nm", 0, "2"), ("p1", 2), ("pj", 0), ("kvs",), ("o2", 5), ("p0", 3), ("o2", 4), ("p1b", 2), ("os", 5),
-    ("o1b", 5), ("p1b", 1), ("p0", 4), ("pj", 1), ("oz", 5), ("p1", 3), ("p2", 2), ("bias",), ("p1b", 3),
-    ("p1", 4), ("at", 1), ("p2", 3), ("pj", 2), ("p1b", 4), ("p0", 5), ("p2", 4), ("at", 2), ("pj", 3),
-    ("p1", 5), ("at", 3), ("pj", 4), ("p1b", 5), ("p2", 5), ("at", 4), ("z0",), ("pj", 5, 0, 0),
-    ("pj", 5, 1, 0), ("pj", 5, 0, 1), ("pj", 5, 1, 1), ("at", 5),
+    ("halo",), ("ox", 1), ("o1", 1), ("oz", 0), ("hw",), ("ox", 3), ("ao", 1), ("ao", 3), ("ox", 2), ("o1", 3),
+    ("ay",), ("p0", 0), ("oz", 1), ("ao", 2), ("ox", 4), ("os", 4), ("ox", 5), ("o1", 4), ("o1", 2), ("o1b", 3),
+    ("af", 0), ("az", 1), ("ss",), ("ox", 0), ("p0", 1), ("o1", 5), ("af", 1), ("az", 3), ("oz", 2), ("p1", 1),
+    ("o2", 4), ("bias",), ("p1", 0), ("o1b", 0), ("sc",), ("az", 2), ("o1b", 5), ("o1", 0), ("o2", 5),
+    ("nm", 0, "2"), ("oz", 3), ("os", 5), ("p0", 2), ("o2", 2), ("p1b", 1), ("p2", 0), ("af", 3),
+    ("nm", 2, "0"), ("os", 3), ("p1b", 0), ("os", 2), ("nm", 0, "0"), ("o1b", 2), ("o2", 0), ("os", 1),
+    ("o1b", 1), ("o1b", 4), ("af", 2), ("oz", 4), ("p1", 2), ("nm", 1, "0"), ("nm", 0, "o"), ("nm", 0, "d"),
+    ("nm", 2, "o"), ("p1b", 2), ("o2", 1), ("os", 0), ("nm", 1, "2"), ("nm", 3, "o"), ("nm", 1, "o"), ("oz", 5),
+    ("nm", 1, "d"), ("nm", 3, "d"), ("nm", 2, "d"), ("nm", 3, "2"), ("p0", 3), ("nm", 3, "0"), ("p2", 2),
+    ("p2", 1), ("nm", 2, "2"), ("pj", 0), ("kvs",), ("p1", 3), ("p1b", 3), ("pj", 1), ("p0", 4), ("p0", 5),
+    ("o2", 3), ("p2", 3), ("pj", 2), ("p1", 4), ("pj", 3), ("p1", 5), ("p1b", 4), ("kw",), ("at", 3),
+    ("p1b", 5), ("p2", 4), ("at", 2), ("at", 1), ("p2", 5), ("pj", 4), ("z0",), ("at", 4), ("pj", 5, 1, 0),
+    ("pj", 5, 0, 0), ("pj", 5, 1, 1), ("pj", 5, 0, 1), ("at", 5),
 )
 
 
 def kernel(len_ref, x_ref, gain_ref, wq_ref, wkv_ref, head_ref, out_ref, *scratch):
     w = scratch[:CHUNKS]
     (
-        kvw, xs, ext, halo, a, an, sq, scale, bias, acc, kv, oacc, parts,
+        kvw, xs, ext, halo, a, an, sq, scale, bias, acc, qb, kv, oacc, parts,
         x_sem, w_sem, ws, wr, a_s, a_r, h_s, h_r, kv_s, kv_r, p_s, p_r, q_s, q_r,
     ) = scratch[CHUNKS:]
     y = lax.axis_index("sec")
@@ -247,6 +247,10 @@
         return carry
 
 
+    def keep(n):
+        base = sum(COLS[1:n])
+        qb[:, base : base + COLS[n]] = acc[:, : COLS[n]].astype(jnp.bfloat16)
+
     def attend(n):
         lanes = [slice(j, j + HEAD_SIZE) for j in range(0, COLS[n], HEAD_SIZE)]
         base = sum(COLS[1:n])
@@ -254,9 +258,9 @@
         for i in range(3):
             rows = slice(i * BLOCK, (i + 1) * BLOCK)
             window = slice(i * BLOCK, (i + 4) * BLOCK)
-            q = jnp.concatenate([acc[rows, j] for j in lanes], axis=0)
+            q = jnp.concatenate([qb[rows, base + j.start : base + j.stop] for j in lanes], axis=0)
             s = lax.dot_general(
-                q.astype(jnp.bfloat16), kv[window, :HEAD_SIZE],
+                q, kv[window, :HEAD_SIZE],
                 (((1,), (1,)), ((), ())), preferred_element_type=jnp.float32,
             )
             s = s * (math.log2(math.e) / math.sqrt(HEAD_SIZE))
@@ -372,6 +376,8 @@
                     return carry
 
                 lax.fori_loop(0, 4, step, 0)
+                if n > 0:
+                    keep(n)
                 return
             h_ = h + a_ - 2 * h * a_
             c_ = c + b_ - 2 * c * b_
@@ -386,13 +392,16 @@
         def z0():
             acc[...] = jnp.zeros_like(acc)
 
+        def kw():
+            kv_copy.wait_recv()
+
         def kvs():
             kv[LOCAL_TOKENS:] = acc[...].astype(jnp.bfloat16)
             kv_copy.start()
 
         def at(n):
-            if n == 1:
-                kv_copy.wait_recv()
+            if n == CHUNKS - 1:
+                keep(n)
             attend(n)
 
     for name, *args in ORDER:
@@ -449,6 +458,7 @@
             pltpu.VMEM((LOCAL_TOKENS, 128), f32),
             pltpu.VMEM((3, BLOCK, 4 * BLOCK), f32),
             pltpu.VMEM((LOCAL_TOKENS, max(COLS)), f32),
+            pltpu.VMEM((LOCAL_TOKENS, sum(COLS[1:])), bf16),
             pltpu.VMEM((2 * LOCAL_TOKENS, 2 * HEAD_SIZE), bf16),
             pltpu.VMEM((LOCAL_TOKENS, HEAD_SIZE), f32),
             pltpu.VMEM((16, 1, LOCAL_TOKENS), f32),

time: 158 us -> 154 us (0.975)
  Pallas kernels: 153 us -> 150 us
    pallas_call x1, Pallas kernels: 153 us -> 150 us  [local(): pl.pallas_call(kernel, out_shape=jax.ShapeDtypeStruct((SEC + 1, LOCAL_TOK...]
where the time goes in v3:
time: 154 us; the launch traced here: 153 us
  Pallas kernels  150 us (97%)
  local copies, waits for them, and re-layouts  2.6 us (2%)
    pallas_call x1, Pallas kernels, local(): pl.pallas_call(kernel, out_shape=jax.ShapeDtypeStruct((SEC + 1, LOCAL_TOK...  150 us

profile of v3, /device:TPU:4, one launch (start us, length us, event | category | flops | bytes accessed | tf_op | source)
XLA Modules:
  0.0 153.3 jit_solution(9129664292650256474)
XLA Ops:
  0.6 150.1 %score_rollouts.1 = f32[5,384]{1,0:T(8,128)} custom-call(s32[32]{0:T(128)} %len_ref.1, bf16[2,384,2048]{2,1,0:T(8,128)(2,1)} %x_ref.1, f32[1,8192]{1,0:T(1,128)} %gain_ref.1, bf16[1,512,1024]{2,1,0:T(8,128)(2,1)} %wq_ref.1, bf16[1,512,2,128]{3,2,1,0:T(2,128)(2,1)} %wkv_ref.1, f32[1,1024]{1,0:T(1,128)} %head_ref.1), custom_call_target="tpu_custom_call" | custom-call | tf_op jit(solution)/shard_map/score_rollouts/pallas_call | solution.py:444
  150.7 1.3 slice_reduce_fusion
  152.0 1.3 slice.6

commit v4 on v3

--- a/solution.py
+++ b/solution.py
@@ -19,26 +19,25 @@
 TP = 4
 WIDTH = 8192
 PIECE = 512
-COLS = (256, 256, 256, 256, 128, 128)
+COLS = (256, 256, 256, 256, 256)
 CHUNKS = len(COLS)
 BLOCK = 128
 NEG = -1e30
 SENDS = 15
 
 ORDER = (
-    ("halo",), ("ox", 1), ("o1", 1), ("oz", 0), ("hw",), ("ox", 3), ("ao", 1), ("ao", 3), ("ox", 2), ("o1", 3),
-    ("ay",), ("p0", 0), ("oz", 1), ("ao", 2), ("ox", 4), ("os", 4), ("ox", 5), ("o1", 4), ("o1", 2), ("o1b", 3),
-    ("af", 0), ("az", 1), ("ss",), ("ox", 0), ("p0", 1), ("o1", 5), ("af", 1), ("az", 3), ("oz", 2), ("p1", 1),
-    ("o2", 4), ("bias",), ("p1", 0), ("o1b", 0), ("sc",), ("az", 2), ("o1b", 5), ("o1", 0), ("o2", 5),
-    ("nm", 0, "2"), ("oz", 3), ("os", 5), ("p0", 2), ("o2", 2), ("p1b", 1), ("p2", 0), ("af", 3),
-    ("nm", 2, "0"), ("os", 3), ("p1b", 0), ("os", 2), ("nm", 0, "0"), ("o1b", 2), ("o2", 0), ("os", 1),
-    ("o1b", 1), ("o1b", 4), ("af", 2), ("oz", 4), ("p1", 2), ("nm", 1, "0"), ("nm", 0, "o"), ("nm", 0, "d"),
-    ("nm", 2, "o"), ("p1b", 2), ("o2", 1), ("os", 0), ("nm", 1, "2"), ("nm", 3, "o"), ("nm", 1, "o"), ("oz", 5),
-    ("nm", 1, "d"), ("nm", 3, "d"), ("nm", 2, "d"), ("nm", 3, "2"), ("p0", 3), ("nm", 3, "0"), ("p2", 2),
-    ("p2", 1), ("nm", 2, "2"), ("pj", 0), ("kvs",), ("p1", 3), ("p1b", 3), ("pj", 1), ("p0", 4), ("p0", 5),
-    ("o2", 3), ("p2", 3), ("pj", 2), ("p1", 4), ("pj", 3), ("p1", 5), ("p1b", 4), ("kw",), ("at", 3),
-    ("p1b", 5), ("p2", 4), ("at", 2), ("at", 1), ("p2", 5), ("pj", 4), ("z0",), ("at", 4), ("pj", 5, 1, 0),
-    ("pj", 5, 0, 0), ("pj", 5, 1, 1), ("pj", 5, 0, 1), ("at", 5),
+    ("halo",), ("os", 4), ("ox", 4), ("ox", 2), ("ox", 1), ("oz", 1), ("ox", 0), ("oz", 0), ("hw",), ("ay",),
+    ("o1", 4), ("o1", 0), ("os", 0), ("ao", 3), ("ao", 1), ("af", 0), ("p0", 0), ("o1b", 2), ("ao", 2),
+    ("o2", 4), ("o1b", 0), ("o1b", 1), ("o1", 1), ("o1", 2), ("p0", 1), ("az", 1), ("os", 1), ("bias",),
+    ("p1b", 0), ("os", 3), ("ss",), ("az", 3), ("af", 1), ("ox", 3), ("os", 2), ("p1", 1), ("oz", 2), ("o2", 0),
+    ("p1", 0), ("o1", 3), ("sc",), ("az", 2), ("oz", 3), ("o2", 2), ("o2", 1), ("p0", 2), ("af", 2),
+    ("nm", 1, "2"), ("nm", 2, "0"), ("o1b", 4), ("nm", 0, "0"), ("af", 3), ("nm", 0, "o"), ("nm", 2, "o"),
+    ("o2", 3), ("nm", 1, "d"), ("nm", 0, "d"), ("oz", 4), ("p1b", 1), ("p2", 0), ("nm", 1, "0"), ("p2", 1),
+    ("p1", 2), ("nm", 3, "d"), ("nm", 3, "o"), ("nm", 3, "0"), ("p0", 3), ("nm", 0, "2"), ("nm", 2, "d"),
+    ("nm", 2, "2"), ("o1b", 3), ("p2", 2), ("nm", 3, "2"), ("p1b", 2), ("nm", 1, "o"), ("pj", 0), ("p1", 3),
+    ("kvs",), ("pj", 1), ("p0", 4), ("p1b", 3), ("p2", 3), ("pj", 2), ("p1", 4), ("pj", 3), ("z0",), ("kw",),
+    ("pj", 4, 0, 0), ("at", 1), ("p1b", 4), ("p2", 4), ("pj", 4, 1, 0), ("at", 2), ("pj", 4, 0, 1), ("at", 3),
+    ("pj", 4, 1, 1), ("at", 4),
 )
 
 

time: 154 us -> 150 us (0.974)
  Pallas kernels: 150 us -> 147 us
    pallas_call x1, Pallas kernels: 150 us -> 147 us  [local(): pl.pallas_call(kernel, out_shape=jax.ShapeDtypeStruct((SEC + 1, LOCAL_TOK...]
where the time goes in v4:
time: 150 us
  Pallas kernels  147 us (98%)
  local copies, waits for them, and re-layouts  2.6 us (2%)
    pallas_call x1, Pallas kernels, local(): pl.pallas_call(kernel, out_shape=jax.ShapeDtypeStruct((SEC + 1, LOCAL_TOK...  147 us

profile of v4, /device:TPU:4, one launch (start us, length us, event | category | flops | bytes accessed | tf_op | source)
XLA Modules:
  0.0 149.8 jit_solution(10881428629647380770)
XLA Ops:
  0.6 146.6 %score_rollouts.1 = f32[5,384]{1,0:T(8,128)} custom-call(s32[32]{0:T(128)} %len_ref.1, bf16[2,384,2048]{2,1,0:T(8,128)(2,1)} %x_ref.1, f32[1,8192]{1,0:T(1,128)} %gain_ref.1, bf16[1,512,1024]{2,1,0:T(8,128)(2,1)} %wq_ref.1, bf16[1,512,2,128]{3,2,1,0:T(2,128)(2,1)} %wkv_ref.1, f32[1,1024]{1,0:T(1,128)} %head_ref.1), custom_call_target="tpu_custom_call" | custom-call | tf_op jit(solution)/shard_map/score_rollouts/pallas_call | solution.py:443
  147.2 1.3 slice_reduce_fusion
  148.5 1.3 slice.6

commit v5 on v4

--- a/solution.py
+++ b/solution.py
@@ -408,29 +408,31 @@
 
     parts[group] = jnp.sum(oacc[...].T, axis=0, keepdims=True)
     parts_start()
+
+    for n in range(CHUNKS):
+        def drain(i, carry):
+            wcopy(n, tok, i, to_sib).wait_send()
+            return carry
+
+        lax.fori_loop(0, SENDS, drain, 0)
+
+    def drain_a(i, carry):
+        acopy(mine, i, to_yd).wait_send()
+        return carry
+
+    lax.fori_loop(0, 15, drain_a, 0)
+    to_right.wait_send()
+    to_left.wait_send()
+    kv_copy.wait_send()
+
+    squares_drain()
+
     parts_wait()
     score = [(parts[4 * s] + parts[4 * s + 1]) + (parts[4 * s + 2] + parts[4 * s + 3]) for s in range(SEC)]
     for s in range(SEC):
         out_ref[s : s + 1] = score[s]
     out_ref[SEC : SEC + 1] = score[1] - score[2] - KL_WEIGHT * (score[3] - score[0])
 
-    for n in range(CHUNKS):
-        def drain(i, carry):
-            wcopy(n, tok, i, to_sib).wait_send()
-            return carry
-
-        lax.fori_loop(0, SENDS, drain, 0)
-
-    def drain_a(i, carry):
-        acopy(mine, i, to_yd).wait_send()
-        return carry
-
-    lax.fori_loop(0, 15, drain_a, 0)
-    to_right.wait_send()
-    to_left.wait_send()
-    kv_copy.wait_send()
-
-    squares_drain()
     parts_drain()
 
 

time: 150 us -> 149 us (level)
  no operation moved by 1% of the time
where the time goes in v5:
time: 149 us
  Pallas kernels  146 us (98%)
  local copies, waits for them, and re-layouts  2.6 us (2%)
    pallas_call x1, Pallas kernels, local(): pl.pallas_call(kernel, out_shape=jax.ShapeDtypeStruct((SEC + 1, LOCAL_TOK...  146 us

profile of v5, /device:TPU:4, one launch (start us, length us, event | category | flops | bytes accessed | tf_op | source)
XLA Modules:
  0.0 149.1 jit_solution(411846864894673768)
XLA Ops:
  0.6 145.8 %score_rollouts.1 = f32[5,384]{1,0:T(8,128)} custom-call(s32[32]{0:T(128)} %len_ref.1, bf16[2,384,2048]{2,1,0:T(8,128)(2,1)} %x_ref.1, f32[1,8192]{1,0:T(1,128)} %gain_ref.1, bf16[1,512,1024]{2,1,0:T(8,128)(2,1)} %wq_ref.1, bf16[1,512,2,128]{3,2,1,0:T(2,128)(2,1)} %wkv_ref.1, f32[1,1024]{1,0:T(1,128)} %head_ref.1), custom_call_target="tpu_custom_call" | custom-call | tf_op jit(solution)/shard_map/score_rollouts/pallas_call | solution.py:445
  146.5 1.3 slice_reduce_fusion
  147.8 1.3 slice.6
